TPU v7x, 512 devices: a whole 4x8x8 slice. The times are simulated.
512 devices in a mesh: col: 64 (over y, z_lo, core), row: 8 (over x, z_hi).
Axes of the slice: x: 4, y: 8, z: 8 (z_hi: 2, z_lo: 4; z = z_hi * 4 + z_lo), core: 2. Of those that a mesh axis runs over, the one named last changes fastest.
Arguments:
- field: bfloat16 [128, 1024, 128], P('row', 'col'), may hold values from -6 to 6
- cotangent: bfloat16 [128, 1024, 128], P('row', 'col'), may hold values from -6 to 6
- w_first: bfloat16 [3, 3, 128, 128], replicated, may hold values from -0.1875 to 0.1875
- w_down: bfloat16 [3, 3, 128, 256], replicated, may hold values from -0.1875 to 0.1875
- w_up: bfloat16 [2, 2, 256, 128], replicated, may hold values from -0.375 to 0.375
- offsets: int32 [8, 64, 2], replicated, may hold values from -8 to 8
- blend_table: int32 [32, 32], replicated, may hold values from 1 to 16
Outputs:
- blended: bfloat16 [128, 1024, 128], P('row', 'col')
- field_grad: float32 [128, 1024, 128], P('row', 'col')
- grad_first: float32 [3, 3, 128, 128], replicated
- grad_down: float32 [3, 3, 128, 256], replicated
- grad_up: float32 [2, 2, 256, 128], replicated
Inputs may be any that keep to these rules, and one draw needn't show every extreme that they name: `offsets`: A patch's first cell lies 8 cells minus its offset before its tile's first cell on each axis.
All inputs are finite; a program needn't handle non-finite values.
Results may differ from a plain program's by a relative error of at most 0.015.
Values may be sent and summed in bfloat16 or wider, within the bound.
No kernel may reach another device: no remote copies, remote signals or barrier semaphores. Data moves between devices by JAX's collectives and lax.ppermute only.
A program may use at most 64 MiB of HBM per device.

v0:
```python
import math
import jax
import jax.numpy as jnp
from jax import lax
from jax.sharding import PartitionSpec as P

MARGIN = 8


def passed_along(block, axis, distance):
    devices = range(lax.axis_size(axis))
    route = [(i - distance, i) for i in devices if i - distance in devices]
    return lax.ppermute(block, axis, route)


def extended(x, sides, width):
    for axis, dim in sides:
        size, length = (lax.axis_size(axis), x.shape[dim])
        up = [(i, (i + 1) % size) for i in range(size - 1)]
        down = [(j, i) for i, j in up]
        last = lax.slice_in_dim(x, length - width, length, axis=dim)
        leading = lax.slice_in_dim(x, 0, width, axis=dim)
        before = lax.ppermute(last, axis, up)
        after = lax.ppermute(leading, axis, down)
        x = jnp.concatenate([before, x, after], axis=dim)
    return x


def conv_same(inputs, kernel):
    rows, cols, chans = inputs.shape
    padded = jnp.pad(inputs, ((1, 1), (1, 1), (0, 0)))
    total = jnp.zeros((rows * cols, kernel.shape[3]), jnp.float32)
    for row_tap in range(3):
        for col_tap in range(3):
            window = padded[row_tap : row_tap + rows, col_tap : col_tap + cols].reshape(
                rows * cols, chans
            )
            total = total + jnp.dot(
                window, kernel[row_tap, col_tap], preferred_element_type=jnp.float32
            )
    return total.reshape(rows, cols, kernel.shape[3])


def conv_down(inputs, kernel):
    rows, cols, chans = inputs.shape
    padded = jnp.pad(inputs, ((1, 1), (1, 1), (0, 0)))
    half_r = rows // 2
    half_c = cols // 2
    total = jnp.zeros((half_r * half_c, kernel.shape[3]), jnp.float32)
    for row_tap in range(3):
        for col_tap in range(3):
            window = padded[row_tap : row_tap + rows : 2, col_tap : col_tap + cols : 2].reshape(
                half_r * half_c, chans
            )
            total = total + jnp.dot(
                window, kernel[row_tap, col_tap], preferred_element_type=jnp.float32
            )
    return total.reshape(half_r, half_c, kernel.shape[3])


def conv_up(inputs, kernel):
    rows, cols, chans = inputs.shape
    flat = inputs.reshape(rows * cols, chans)
    lines = []
    for row_tap in range(2):
        pieces = []
        for col_tap in range(2):
            pieces.append(
                jnp.dot(flat, kernel[row_tap, col_tap], preferred_element_type=jnp.float32).reshape(
                    rows, cols, kernel.shape[3]
                )
            )
        lines.append(jnp.stack(pieces, axis=2))
    return jnp.stack(lines, axis=1).reshape(2 * rows, 2 * cols, kernel.shape[3])


def patch_net(patch, w_first, w_down, w_up):
    hidden = jax.nn.silu(conv_same(patch, w_first)).astype(jnp.bfloat16)
    lower = jax.nn.silu(conv_down(hidden, w_down)).astype(jnp.bfloat16)
    return hidden.astype(jnp.float32) + conv_up(lower, w_up)


def return_margins(canvas, tile_h, tile_w, edge):
    summed = canvas
    for heading in (1, -1):
        strip = canvas[tile_h + edge :] if heading == 1 else canvas[:edge]
        arrived = passed_along(strip.astype(jnp.bfloat16), "row", heading).astype(strip.dtype)
        if heading == 1:
            summed = summed.at[edge : 2 * edge].add(arrived)
        else:
            summed = summed.at[tile_h : tile_h + edge].add(arrived)
    middle = summed[edge : tile_h + edge]
    result = middle
    for heading in (1, -1):
        strip = middle[:, tile_w + edge :] if heading == 1 else middle[:, :edge]
        arrived = passed_along(strip.astype(jnp.bfloat16), "col", heading).astype(strip.dtype)
        if heading == 1:
            result = result.at[:, edge : 2 * edge].add(arrived)
        else:
            result = result.at[:, tile_w : tile_w + edge].add(arrived)
    return result[:, edge : tile_w + edge]


def weight_total(offsets, table_f, row_at, col_at, rows_n, cols_n, tile_h, tile_w, lead, reach):
    patch_h, patch_w = table_f.shape
    total = jnp.zeros((tile_h + 2 * lead, tile_w + 2 * lead), jnp.float32)
    for row_step in range(-reach, reach + 1):
        for col_step in range(-reach, reach + 1):
            near_row = row_at + row_step
            near_col = col_at + col_step
            inside = (
                (near_row >= 0) & (near_row < rows_n) & (near_col >= 0) & (near_col < cols_n)
            ).astype(jnp.float32)
            shift_pair = offsets[
                jnp.clip(near_row, 0, rows_n - 1), jnp.clip(near_col, 0, cols_n - 1)
            ]
            top = row_step * tile_h - MARGIN + shift_pair[0] + lead
            left = col_step * tile_w - MARGIN + shift_pair[1] + lead
            pick_rows = (
                jnp.arange(tile_h + 2 * lead)[:, None] - top == jnp.arange(patch_h)[None, :]
            ).astype(jnp.float32)
            pick_cols = (
                jnp.arange(tile_w + 2 * lead)[:, None] - left == jnp.arange(patch_w)[None, :]
            ).astype(jnp.float32)
            placed = jnp.dot(
                jnp.dot(pick_rows, table_f, precision=lax.Precision.HIGHEST),
                pick_cols.T,
                precision=lax.Precision.HIGHEST,
            )
            total = total + inside * placed
    return total


def per_device(field, cotangent, w_first, w_down, w_up, offsets, blend_table):
    tile_h, tile_w, chans = field.shape
    patch_h, patch_w = blend_table.shape
    edge = 2 * MARGIN
    rows_n = lax.axis_size("row")
    cols_n = lax.axis_size("col")
    row_at = lax.axis_index("row")
    col_at = lax.axis_index("col")
    table_f = blend_table.astype(jnp.float32)
    grown = extended(field, (("row", 0), ("col", 1)), edge)
    own_shift = offsets[row_at, col_at]
    start_r = MARGIN + own_shift[0]
    start_c = MARGIN + own_shift[1]
    zero = jnp.int32(0)
    patch = lax.dynamic_slice(grown, (start_r, start_c, zero), (patch_h, patch_w, chans))
    out_patch, back = jax.vjp(patch_net, patch, w_first, w_down, w_up)
    empty = jnp.zeros((tile_h + 2 * edge, tile_w + 2 * edge, chans), jnp.float32)
    canvas = lax.dynamic_update_slice(
        empty, table_f[:, :, None] * out_patch, (start_r, start_c, zero)
    )
    numer = return_margins(canvas, tile_h, tile_w, edge)
    weight_sum = weight_total(
        offsets, table_f, row_at, col_at, rows_n, cols_n, tile_h, tile_w, 0, 1
    )
    ratio = cotangent.astype(jnp.float32) / weight_sum[:, :, None]
    ratio_grown = extended(ratio.astype(jnp.bfloat16), (("row", 0), ("col", 1)), edge).astype(
        ratio.dtype
    )
    blended = (numer / weight_sum[:, :, None]).astype(jnp.bfloat16)
    out_grad = table_f[:, :, None] * lax.dynamic_slice(
        ratio_grown, (start_r, start_c, zero), (patch_h, patch_w, chans)
    )
    d_patch, d_first, d_down, d_up = back(out_grad)
    d_canvas = lax.dynamic_update_slice(
        empty, d_patch.astype(jnp.float32), (start_r, start_c, zero)
    )
    field_grad = return_margins(d_canvas, tile_h, tile_w, edge)
    g_first, g_down, g_up = lax.psum(
        (d_first.astype(jnp.float32), d_down.astype(jnp.float32), d_up.astype(jnp.float32)),
        ("col", "row"),
    )
    scale = 1.0 / math.sqrt(tile_h * rows_n * tile_w * cols_n)
    return (blended, field_grad, g_first * scale, g_down * scale, g_up * scale)


def solution(mesh):
    return jax.shard_map(
        per_device,
        mesh=mesh,
        in_specs=(P("row", "col", None), P("row", "col", None), P(), P(), P(), P(), P()),
        out_specs=(P("row", "col", None), P("row", "col", None), P(), P(), P()),
        check_vma=False,
    )
```

profile of v0, /device:TPU:17, one launch (start us, length us, event | category | flops | bytes accessed | tf_op | source)
XLA Modules:
  0.0 498.5 jit_solution(4310469566527345241)
XLA Ops:
  7.2 10.6 %collective-permute-start = (bf16[16,16,128]{2,1,0:T(8,128)(2,1)}, bf16[16,16,128]{2,1,0:T(8,128)(2,1)S(1)}, u32[]{:S(2)}, u32[]{:S(2)}) collective-permute-start(bf16[16,16,128]{2,1,0:T(8,128)(2,1)} %param.23), channel_id=1, source_target_pairs={{0,1},{1,2},{2,3},{3,4},{4,5},{5,6},{6,7},{8,9},{9,10},{10,11},{11... | collective-permute-start | bytes 196616 | tf_op jit(solution)/shard_map/ppermute | solution.py:23
  17.9 1.3 collective-permute-start.1
  19.2 1.0 constant_dynamic-slice_fusion
  23.4 0.9 fusion.167
  24.3 0.9 fusion.168
  26.5 0.9 fusion.169
  29.4 0.9 fusion.170
  31.7 0.9 fusion.171
  34.5 0.9 fusion.172
  36.8 0.9 fusion.173
  39.6 0.9 fusion.174
  41.9 0.9 fusion.175
  45.4 3.9 collective-permute-start.2
  49.3 1.9 collective-permute-start.3
  51.4 8.1 %collective-permute-start.8 = (bf16[16,16,128]{2,1,0:T(8,128)(2,1)S(1)}, bf16[16,16,128]{2,1,0:T(8,128)(2,1)S(1)}, u32[]{:S(2)}, u32[]{:S(2)}) collective-permute-start(bf16[16,16,128]{2,1,0:T(8,128)(2,1)S(1)} %divide_convert_fusion), channel_id=1, source_target_pairs={{0,1},{1,2},{2,3},{3,4},{4,5},{5,6},{6,7},{8,9},{9,10},{10,11},{11... | collective-permute-start | bytes 196616 | tf_op jit(solution)/shard_map/ppermute | solution.py:23
  59.5 1.3 collective-permute-start.9
  63.4 5.0 %collective-permute-done.9 = bf16[16,16,128]{2,1,0:T(8,128)(2,1)S(1)} collective-permute-done((bf16[16,16,128]{2,1,0:T(8,128)(2,1)S(1)}, bf16[16,16,128]{2,1,0:T(8,128)(2,1)S(1)}, u32[]{:S(2)}, u32[]{:S(2)}) %collective-permute-start.9) | collective-permute-done | bytes 65568 | tf_op jit(solution)/shard_map/ppermute | solution.py:24
  69.2 5.7 %collective-permute-start.10 = (bf16[48,16,128]{2,1,0:T(8,128)(2,1)}, bf16[48,16,128]{2,1,0:T(8,128)(2,1)}, u32[]{:S(2)}, u32[]{:S(2)}) collective-permute-start(bf16[48,16,128]{2,1,0:T(8,128)(2,1)} %pad_maximum_fusion.1), channel_id=1, source_target_pairs={{0,8},{8,16},{16,24},{24,32},{32,40},{40,48},{48,56},{56,64},{64,7... | collective-permute-start | bytes 589832 | tf_op jit(solution)/shard_map/ppermute | solution.py:23
  74.9 2.8 collective-permute-start.11
  88.6 2.3 convert_multiply_fusion.2
  107.4 5.6 %pad.156 = bf16[34,34,128]{2,1,0:T(8,128)(2,1)S(1)} pad(bf16[16,16,128]{2,1,0:T(8,128)(2,1)} %bitcast.505, bf16[]{:T(256)} %constant.241.clone.1), padding=2_1_1x0_3_1x0_0_0 | pad | bytes 361474 | tf_op jit(solution)/shard_map/transpose(jvp())/pad | solution.py:52
  113.0 8.5 %pad.345 = bf16[33,33,128]{2,1,0:T(8,128)(2,1)} pad(bf16[16,16,128]{2,1,0:T(8,128)(2,1)} %bitcast.504, bf16[]{:T(256)} %constant.241.clone.1), padding=0_2_1x0_2_1x0_0_0 | pad | bytes 344322
  121.5 8.5 %pad.348 = bf16[32,33,128]{2,1,0:T(8,128)(2,1)} pad(bf16[16,16,128]{2,1,0:T(8,128)(2,1)} %bitcast.511, bf16[]{:T(256)} %constant.241.clone.1), padding=0_1_1x0_2_1x0_0_0 | pad | bytes 335874
  130.0 8.4 %pad.346 = bf16[33,32,128]{2,1,0:T(8,128)(2,1)} pad(bf16[16,16,128]{2,1,0:T(8,128)(2,1)} %bitcast.510, bf16[]{:T(256)} %constant.241.clone.1), padding=0_2_1x0_1_1x0_0_0 | pad | bytes 335874
  138.4 8.4 %pad.347 = bf16[33,32,128]{2,1,0:T(8,128)(2,1)} pad(bf16[16,16,128]{2,1,0:T(8,128)(2,1)} %bitcast.509, bf16[]{:T(256)} %constant.241.clone.1), padding=0_2_1x1_0_1x0_0_0 | pad | bytes 335874
  146.8 8.4 %pad.214 = bf16[32,32,128]{2,1,0:T(8,128)(2,1)} pad(bf16[16,16,128]{2,1,0:T(8,128)(2,1)} %bitcast.503, bf16[]{:T(256)} %constant.241.clone.1), padding=0_1_1x1_0_1x0_0_0 | pad | bytes 327682 | tf_op jit(solution)/shard_map/transpose(jvp(jit(_pad)))/pad | solution.py:46
  155.2 5.6 %pad.215 = bf16[32,32,128]{2,1,0:T(8,128)(2,1)} pad(bf16[16,16,128]{2,1,0:T(8,128)(2,1)S(1)} %bitcast.502, bf16[]{:T(256)} %constant.241.clone.1), padding=0_1_1x0_1_1x0_0_0 | pad | bytes 327682 | tf_op jit(solution)/shard_map/transpose(jvp(jit(_pad)))/pad | solution.py:46
  162.0 1.7 fusion.52
  164.5 0.9 fusion.38
  166.3 0.9 fusion.40
  167.2 0.9 fusion.41
  172.8 1.3 dynamic_update_slice.7
  174.9 4.2 collective-permute-start.12
  179.1 1.3 collective-permute-start.13
  180.4 1.3 dynamic_update_slice.6
  182.7 8.6 %collective-permute-start.4 = (bf16[16,48,128]{2,1,0:T(8,128)(2,1)}, bf16[16,48,128]{2,1,0:T(8,128)(2,1)}, u32[]{:S(2)}, u32[]{:S(2)}) collective-permute-start(bf16[16,48,128]{2,1,0:T(8,128)(2,1)} %get-tuple-element.110), channel_id=1, source_target_pairs={{0,1},{1,2},{2,3},{3,4},{4,5},{5,6},{6,7},{8,9},{9,10},{10,11},{11... | collective-permute-start | bytes 589832 | tf_op jit(solution)/shard_map/ppermute | solution.py:13
  191.2 1.3 collective-permute-start.5
  194.6 1.2 add_convert_fusion
  195.8 11.9 %collective-permute-done.5 = bf16[16,48,128]{2,1,0:T(8,128)(2,1)} collective-permute-done((bf16[16,48,128]{2,1,0:T(8,128)(2,1)S(1)}, bf16[16,48,128]{2,1,0:T(8,128)(2,1)}, u32[]{:S(2)}, u32[]{:S(2)}) %collective-permute-start.5) | collective-permute-done | bytes 196640 | tf_op jit(solution)/shard_map/ppermute | solution.py:13
  207.6 1.1 fusion.205
  208.7 12.5 %collective-permute-start.6 = (bf16[16,16,128]{2,1,0:T(8,128)(2,1)S(1)}, bf16[16,16,128]{2,1,0:T(8,128)(2,1)S(1)}, u32[]{:S(2)}, u32[]{:S(2)}) collective-permute-start(bf16[16,16,128]{2,1,0:T(8,128)(2,1)S(1)} %get-tuple-element.128), channel_id=1, source_target_pairs={{0,8},{8,16},{16,24},{24,32},{32,40},{40,48},{48,56},{56,64},{64,7... | collective-permute-start | bytes 196616 | tf_op jit(solution)/shard_map/ppermute | solution.py:13
  221.3 1.9 collective-permute-start.7
  223.2 1.1 fusion.203
  224.3 3.6 collective-permute-start.14
  228.0 1.9 collective-permute-start.15
  230.7 3.3 collective-permute-done.15
  234.7 252.5 %all-reduce.45.cloned.1.call-done = (f32[3,3,128,128]{3,2,1,0:T(8,128)}, f32[3,3,128,256]{3,2,1,0:T(8,128)}, f32[2,2,256,128]{3,2,1,0:T(8,128)}) async-done(((f32[3,3,128,128]{3,2,1,0:T(8,128)}, f32[3,3,128,256]{3,2,1,0:T(8,128)}, f32[2,2,256,128]{3,2,1,0:T(8,128)}), (f32[3,3,128,128]{3,2,1,0:T(8,128)}, f32[3,3,128,256]{3,2,1,0:T(8,128)}, f32[2,2,256,128]{3,2,1,0:T(8,128)})) %all-reduce.45.cloned.1.call-update) | async-done | bytes 2293776 | tf_op jit(solution)/shard_map/psum | solution.py:171
  487.1 2.4 broadcast_multiply_fusion
  (244 shorter events, 47.3 us)
Async XLA Ops:
  7.2 38.1 %copy-start.35 = (bf16[16,16,128]{2,1,0:T(8,128)(2,1)S(1)}, bf16[16,16,128]{2,1,0:T(8,128)(2,1)}, u32[]{:S(2)}) copy-start(bf16[16,16,128]{2,1,0:T(8,128)(2,1)} %param.23) | copy-start | bytes 196612
  7.2 56.2 %copy-start.43 = (s32[32,32]{1,0:T(8,128)S(1)}, s32[32,32]{1,0:T(8,128)}, u32[]{:S(2)}) copy-start(s32[32,32]{1,0:T(8,128)} %param.29) | copy-start | bytes 12292
  7.2 44.1 %copy-start.36 = (bf16[16,16,128]{2,1,0:T(8,128)(2,1)S(1)}, bf16[16,16,128]{2,1,0:T(8,128)(2,1)}, u32[]{:S(2)}) copy-start(bf16[16,16,128]{2,1,0:T(8,128)(2,1)} %param.24) | copy-start | bytes 196612
  7.2 479.9 %all-reduce.45.cloned.1.call-start = ((), (), s32[]{:S(2)}) async-start(), calls=%async_computation | async-start | bytes 4587520 | tf_op jit(solution)/shard_map/psum | solution.py:171
  7.2 38.0 %collective-permute-start = (bf16[16,16,128]{2,1,0:T(8,128)(2,1)}, bf16[16,16,128]{2,1,0:T(8,128)(2,1)S(1)}, u32[]{:S(2)}, u32[]{:S(2)}) collective-permute-start(bf16[16,16,128]{2,1,0:T(8,128)(2,1)} %param.23), channel_id=1, source_target_pairs={{0,1},{1,2},{2,3},{3,4},{4,5},{5,6},{6,7},{8,9},{9,10},{10,11},{11... | collective-permute-start | bytes 196616 | tf_op jit(solution)/shard_map/ppermute | solution.py:23
  17.9 27.5 %collective-permute-start.1 = (bf16[16,16,128]{2,1,0:T(8,128)(2,1)}, bf16[16,16,128]{2,1,0:T(8,128)(2,1)S(1)}, u32[]{:S(2)}, u32[]{:S(2)}) collective-permute-start(bf16[16,16,128]{2,1,0:T(8,128)(2,1)} %param.23), channel_id=1, source_target_pairs={{1,0},{2,1},{3,2},{4,3},{5,4},{6,5},{7,6},{9,8},{10,9},{11,10},{12... | collective-permute-start | bytes 196616 | tf_op jit(solution)/shard_map/ppermute | solution.py:24
  45.4 32.4 %collective-permute-start.2 = (bf16[48,16,128]{2,1,0:T(8,128)(2,1)S(1)}, bf16[48,16,128]{2,1,0:T(8,128)(2,1)S(1)}, u32[]{:S(2)}, u32[]{:S(2)}) collective-permute-start(bf16[48,16,128]{2,1,0:T(8,128)(2,1)S(1)} %constant_dynamic-update-slice_fusion), channel_id=1, source_target_pairs={{0,8},{8,16},{16,24},{24,32},{32,40},{40,48},{48,56},{56,64},{64,7... | collective-permute-start | bytes 589832 | tf_op jit(solution)/shard_map/ppermute | solution.py:23
  49.3 28.4 %collective-permute-start.3 = (bf16[48,16,128]{2,1,0:T(8,128)(2,1)S(1)}, bf16[48,16,128]{2,1,0:T(8,128)(2,1)S(1)}, u32[]{:S(2)}, u32[]{:S(2)}) collective-permute-start(bf16[48,16,128]{2,1,0:T(8,128)(2,1)S(1)} %constant_dynamic-update-slice_fusion), channel_id=1, source_target_pairs={{8,0},{16,8},{24,16},{32,24},{40,32},{48,40},{56,48},{64,56},{72,6... | collective-permute-start | bytes 589832 | tf_op jit(solution)/shard_map/ppermute | solution.py:24
  51.4 12.0 %collective-permute-start.8 = (bf16[16,16,128]{2,1,0:T(8,128)(2,1)S(1)}, bf16[16,16,128]{2,1,0:T(8,128)(2,1)S(1)}, u32[]{:S(2)}, u32[]{:S(2)}) collective-permute-start(bf16[16,16,128]{2,1,0:T(8,128)(2,1)S(1)} %divide_convert_fusion), channel_id=1, source_target_pairs={{0,1},{1,2},{2,3},{3,4},{4,5},{5,6},{6,7},{8,9},{9,10},{10,11},{11... | collective-permute-start | bytes 196616 | tf_op jit(solution)/shard_map/ppermute | solution.py:23
  59.5 9.0 %collective-permute-start.9 = (bf16[16,16,128]{2,1,0:T(8,128)(2,1)S(1)}, bf16[16,16,128]{2,1,0:T(8,128)(2,1)S(1)}, u32[]{:S(2)}, u32[]{:S(2)}) collective-permute-start(bf16[16,16,128]{2,1,0:T(8,128)(2,1)S(1)} %divide_convert_fusion), channel_id=1, source_target_pairs={{1,0},{2,1},{3,2},{4,3},{5,4},{6,5},{7,6},{9,8},{10,9},{11,10},{12... | collective-permute-start | bytes 196616 | tf_op jit(solution)/shard_map/ppermute | solution.py:24
  63.4 14.9 %copy-start.29 = (bf16[16,16,128]{2,1,0:T(8,128)(2,1)}, bf16[16,16,128]{2,1,0:T(8,128)(2,1)S(1)}, u32[]{:S(2)}) copy-start(bf16[16,16,128]{2,1,0:T(8,128)(2,1)S(1)} %collective-permute-done.8) | copy-start | bytes 196612
  68.5 9.9 %copy-start.31 = (bf16[16,16,128]{2,1,0:T(8,128)(2,1)}, bf16[16,16,128]{2,1,0:T(8,128)(2,1)S(1)}, u32[]{:S(2)}) copy-start(bf16[16,16,128]{2,1,0:T(8,128)(2,1)S(1)} %collective-permute-done.9) | copy-start | bytes 196612
  69.2 19.0 %collective-permute-start.10 = (bf16[48,16,128]{2,1,0:T(8,128)(2,1)}, bf16[48,16,128]{2,1,0:T(8,128)(2,1)}, u32[]{:S(2)}, u32[]{:S(2)}) collective-permute-start(bf16[48,16,128]{2,1,0:T(8,128)(2,1)} %pad_maximum_fusion.1), channel_id=1, source_target_pairs={{0,8},{8,16},{16,24},{24,32},{32,40},{40,48},{48,56},{56,64},{64,7... | collective-permute-start | bytes 589832 | tf_op jit(solution)/shard_map/ppermute | solution.py:23
  74.9 13.3 %collective-permute-start.11 = (bf16[48,16,128]{2,1,0:T(8,128)(2,1)}, bf16[48,16,128]{2,1,0:T(8,128)(2,1)}, u32[]{:S(2)}, u32[]{:S(2)}) collective-permute-start(bf16[48,16,128]{2,1,0:T(8,128)(2,1)} %pad_maximum_fusion.1), channel_id=1, source_target_pairs={{8,0},{16,8},{24,16},{32,24},{40,32},{48,40},{56,48},{64,56},{72,6... | collective-permute-start | bytes 589832 | tf_op jit(solution)/shard_map/ppermute | solution.py:24
  80.9 4.0 copy-start
  81.7 3.7 copy-start.16
  83.3 2.3 copy-start.8
  83.7 2.1 copy-start.10
  84.1 1.9 copy-start.12
  95.4 2.5 copy-start.13
  95.4 3.3 copy-start.11
  95.6 3.9 copy-start.9
  174.9 48.3 %collective-permute-start.12 = (bf16[16,48,128]{2,1,0:T(8,128)(2,1)}, bf16[16,48,128]{2,1,0:T(8,128)(2,1)}, u32[]{:S(2)}, u32[]{:S(2)}) collective-permute-start(bf16[16,48,128]{2,1,0:T(8,128)(2,1)} %get-tuple-element.108), channel_id=1, source_target_pairs={{0,1},{1,2},{2,3},{3,4},{4,5},{5,6},{6,7},{8,9},{9,10},{10,11},{11... | collective-permute-start | bytes 589832 | tf_op jit(solution)/shard_map/ppermute | solution.py:13
  179.1 44.1 %collective-permute-start.13 = (bf16[16,48,128]{2,1,0:T(8,128)(2,1)S(1)}, bf16[16,48,128]{2,1,0:T(8,128)(2,1)}, u32[]{:S(2)}, u32[]{:S(2)}) collective-permute-start(bf16[16,48,128]{2,1,0:T(8,128)(2,1)S(1)} %get-tuple-element.109), channel_id=1, source_target_pairs={{1,0},{2,1},{3,2},{4,3},{5,4},{6,5},{7,6},{9,8},{10,9},{11,10},{12... | collective-permute-start | bytes 589832 | tf_op jit(solution)/shard_map/ppermute | solution.py:13
  181.7 10.8 %copy-start.25 = (bf16[1,1,256,128]{3,2,1,0:T(8,128)(2,1)S(1)}, bf16[1,1,256,128]{3,2,1,0:T(8,128)(2,1)}, u32[]{:S(2)}) copy-start(bf16[1,1,256,128]{3,2,1,0:T(8,128)(2,1)} %fusion.14) | copy-start | bytes 196612
  181.7 10.8 %copy-start.26 = (bf16[1,1,256,128]{3,2,1,0:T(8,128)(2,1)S(1)}, bf16[1,1,256,128]{3,2,1,0:T(8,128)(2,1)}, u32[]{:S(2)}) copy-start(bf16[1,1,256,128]{3,2,1,0:T(8,128)(2,1)} %fusion.13) | copy-start | bytes 196612
  181.7 10.8 %copy-start.27 = (bf16[1,1,256,128]{3,2,1,0:T(8,128)(2,1)S(1)}, bf16[1,1,256,128]{3,2,1,0:T(8,128)(2,1)}, u32[]{:S(2)}) copy-start(bf16[1,1,256,128]{3,2,1,0:T(8,128)(2,1)} %fusion.15) | copy-start | bytes 196612
  181.7 10.8 %copy-start.28 = (bf16[1,1,256,128]{3,2,1,0:T(8,128)(2,1)S(1)}, bf16[1,1,256,128]{3,2,1,0:T(8,128)(2,1)}, u32[]{:S(2)}) copy-start(bf16[1,1,256,128]{3,2,1,0:T(8,128)(2,1)} %fusion.16) | copy-start | bytes 196612
  181.8 11.5 %copy-start.37 = (bf16[1,1,128,128]{3,2,1,0:T(8,128)(2,1)S(1)}, bf16[1,1,128,128]{3,2,1,0:T(8,128)(2,1)}, u32[]{:S(2)}) copy-start(bf16[1,1,128,128]{3,2,1,0:T(8,128)(2,1)} %fusion.38) | copy-start | bytes 98308
  181.9 11.5 %copy-start.38 = (bf16[1,1,128,128]{3,2,1,0:T(8,128)(2,1)S(1)}, bf16[1,1,128,128]{3,2,1,0:T(8,128)(2,1)}, u32[]{:S(2)}) copy-start(bf16[1,1,128,128]{3,2,1,0:T(8,128)(2,1)} %fusion.39) | copy-start | bytes 98308
  181.9 11.5 %copy-start.39 = (bf16[1,1,128,128]{3,2,1,0:T(8,128)(2,1)S(1)}, bf16[1,1,128,128]{3,2,1,0:T(8,128)(2,1)}, u32[]{:S(2)}) copy-start(bf16[1,1,128,128]{3,2,1,0:T(8,128)(2,1)} %fusion.40) | copy-start | bytes 98308
  181.9 11.5 %copy-start.40 = (bf16[1,1,128,128]{3,2,1,0:T(8,128)(2,1)S(1)}, bf16[1,1,128,128]{3,2,1,0:T(8,128)(2,1)}, u32[]{:S(2)}) copy-start(bf16[1,1,128,128]{3,2,1,0:T(8,128)(2,1)} %fusion.41) | copy-start | bytes 98308
  181.9 11.5 %copy-start.41 = (bf16[1,1,128,128]{3,2,1,0:T(8,128)(2,1)S(1)}, bf16[1,1,128,128]{3,2,1,0:T(8,128)(2,1)}, u32[]{:S(2)}) copy-start(bf16[1,1,128,128]{3,2,1,0:T(8,128)(2,1)} %fusion.42) | copy-start | bytes 98308
  181.9 11.5 %copy-start.42 = (bf16[1,1,128,128]{3,2,1,0:T(8,128)(2,1)S(1)}, bf16[1,1,128,128]{3,2,1,0:T(8,128)(2,1)}, u32[]{:S(2)}) copy-start(bf16[1,1,128,128]{3,2,1,0:T(8,128)(2,1)} %fusion.43) | copy-start | bytes 98308
  181.9 12.4 %copy-start.17 = (bf16[16,16,128]{2,1,0:T(8,128)(2,1)S(1)}, bf16[16,16,128]{2,1,0:T(8,128)(2,1)}, u32[]{:S(2)}) copy-start(bf16[16,16,128]{2,1,0:T(8,128)(2,1)} %copy-done.16) | copy-start | bytes 196612
  181.9 12.6 %copy-start.19 = (bf16[1,1,128,256]{3,2,1,0:T(8,128)(2,1)S(1)}, bf16[1,1,128,256]{3,2,1,0:T(8,128)(2,1)}, u32[]{:S(2)}) copy-start(bf16[1,1,128,256]{3,2,1,0:T(8,128)(2,1)} %fusion.25) | copy-start | bytes 196612
  181.9 12.6 %copy-start.20 = (bf16[1,1,128,256]{3,2,1,0:T(8,128)(2,1)S(1)}, bf16[1,1,128,256]{3,2,1,0:T(8,128)(2,1)}, u32[]{:S(2)}) copy-start(bf16[1,1,128,256]{3,2,1,0:T(8,128)(2,1)} %fusion.24) | copy-start | bytes 196612
  181.9 12.6 %copy-start.21 = (bf16[1,1,128,256]{3,2,1,0:T(8,128)(2,1)S(1)}, bf16[1,1,128,256]{3,2,1,0:T(8,128)(2,1)}, u32[]{:S(2)}) copy-start(bf16[1,1,128,256]{3,2,1,0:T(8,128)(2,1)} %fusion.23) | copy-start | bytes 196612
  182.0 12.6 %copy-start.22 = (bf16[1,1,128,256]{3,2,1,0:T(8,128)(2,1)S(1)}, bf16[1,1,128,256]{3,2,1,0:T(8,128)(2,1)}, u32[]{:S(2)}) copy-start(bf16[1,1,128,256]{3,2,1,0:T(8,128)(2,1)} %fusion.22) | copy-start | bytes 196612
  182.0 12.6 %copy-start.23 = (bf16[1,1,128,256]{3,2,1,0:T(8,128)(2,1)S(1)}, bf16[1,1,128,256]{3,2,1,0:T(8,128)(2,1)}, u32[]{:S(2)}) copy-start(bf16[1,1,128,256]{3,2,1,0:T(8,128)(2,1)} %fusion.21) | copy-start | bytes 196612
  182.0 12.6 %copy-start.24 = (bf16[1,1,128,256]{3,2,1,0:T(8,128)(2,1)S(1)}, bf16[1,1,128,256]{3,2,1,0:T(8,128)(2,1)}, u32[]{:S(2)}) copy-start(bf16[1,1,128,256]{3,2,1,0:T(8,128)(2,1)} %fusion.20) | copy-start | bytes 196612
  182.7 13.1 %collective-permute-start.4 = (bf16[16,48,128]{2,1,0:T(8,128)(2,1)}, bf16[16,48,128]{2,1,0:T(8,128)(2,1)}, u32[]{:S(2)}, u32[]{:S(2)}) collective-permute-start(bf16[16,48,128]{2,1,0:T(8,128)(2,1)} %get-tuple-element.110), channel_id=1, source_target_pairs={{0,1},{1,2},{2,3},{3,4},{4,5},{5,6},{6,7},{8,9},{9,10},{10,11},{11... | collective-permute-start | bytes 589832 | tf_op jit(solution)/shard_map/ppermute | solution.py:13
  191.2 16.4 %collective-permute-start.5 = (bf16[16,48,128]{2,1,0:T(8,128)(2,1)S(1)}, bf16[16,48,128]{2,1,0:T(8,128)(2,1)}, u32[]{:S(2)}, u32[]{:S(2)}) collective-permute-start(bf16[16,48,128]{2,1,0:T(8,128)(2,1)S(1)} %get-tuple-element.111), channel_id=1, source_target_pairs={{1,0},{2,1},{3,2},{4,3},{5,4},{6,5},{7,6},{9,8},{10,9},{11,10},{12... | collective-permute-start | bytes 589832 | tf_op jit(solution)/shard_map/ppermute | solution.py:13
  208.7 21.2 %collective-permute-start.6 = (bf16[16,16,128]{2,1,0:T(8,128)(2,1)S(1)}, bf16[16,16,128]{2,1,0:T(8,128)(2,1)S(1)}, u32[]{:S(2)}, u32[]{:S(2)}) collective-permute-start(bf16[16,16,128]{2,1,0:T(8,128)(2,1)S(1)} %get-tuple-element.128), channel_id=1, source_target_pairs={{0,8},{8,16},{16,24},{24,32},{32,40},{40,48},{48,56},{56,64},{64,7... | collective-permute-start | bytes 196616 | tf_op jit(solution)/shard_map/ppermute | solution.py:13
  221.3 8.7 %collective-permute-start.7 = (bf16[16,16,128]{2,1,0:T(8,128)(2,1)S(1)}, bf16[16,16,128]{2,1,0:T(8,128)(2,1)S(1)}, u32[]{:S(2)}, u32[]{:S(2)}) collective-permute-start(bf16[16,16,128]{2,1,0:T(8,128)(2,1)S(1)} %get-tuple-element.129), channel_id=1, source_target_pairs={{8,0},{16,8},{24,16},{32,24},{40,32},{48,40},{56,48},{64,56},{72,6... | collective-permute-start | bytes 196616 | tf_op jit(solution)/shard_map/ppermute | solution.py:13
  224.3 6.3 %collective-permute-start.14 = (bf16[16,16,128]{2,1,0:T(8,128)(2,1)S(1)}, bf16[16,16,128]{2,1,0:T(8,128)(2,1)S(1)}, u32[]{:S(2)}, u32[]{:S(2)}) collective-permute-start(bf16[16,16,128]{2,1,0:T(8,128)(2,1)S(1)} %get-tuple-element.126), channel_id=1, source_target_pairs={{0,8},{8,16},{16,24},{24,32},{32,40},{40,48},{48,56},{56,64},{64,7... | collective-permute-start | bytes 196616 | tf_op jit(solution)/shard_map/ppermute | solution.py:13
  228.0 6.0 %collective-permute-start.15 = (bf16[16,16,128]{2,1,0:T(8,128)(2,1)S(1)}, bf16[16,16,128]{2,1,0:T(8,128)(2,1)S(1)}, u32[]{:S(2)}, u32[]{:S(2)}) collective-permute-start(bf16[16,16,128]{2,1,0:T(8,128)(2,1)S(1)} %get-tuple-element.127), channel_id=1, source_target_pairs={{8,0},{16,8},{24,16},{32,24},{40,32},{48,40},{56,48},{64,56},{72,6... | collective-permute-start | bytes 196616 | tf_op jit(solution)/shard_map/ppermute | solution.py:13
  487.1 2.5 copy-start.7
  (13 other events, 15.0 us)
Sparse Core Ops, SparseCore 0:
  195.9 291.1 all-reduce.44
where the time goes:
time: 502 us; the launch traced here: 499 us
  waiting for transfers between devices  273 us (54%)
  starting transfers between devices  71.1 us (14%)
  local copies, waits for them, and re-layouts  70.1 us (14%)
  matrix products  37.5 us (7%)
  between operations  30.1 us (6%)
  other arithmetic  17.1 us (3%)
    psum x1, waiting for transfers between devices, per_device(): lax.psum((d_first.astype(jnp.float32), d_down.astype(jnp.float32), d_up.a...  252 us
    unnamed x94, local copies, waits for them, and re-layouts  37.2 us
    ppermute x8, starting transfers between devices, passed_along(): return lax.ppermute(block, axis, route)  35.3 us
    ppermute x4, starting transfers between devices, extended(): before = lax.ppermute(last, axis, up)  28.4 us
    ppermute x8, waiting for transfers between devices, passed_along(): return lax.ppermute(block, axis, route)  15.2 us
    pad x3, local copies, waits for them, and re-layouts, conv_down(): padded = jnp.pad(inputs, ((1, 1), (1, 1), (0, 0)))  14.1 us
    dot_general x27, matrix products, conv_down(): jnp.dot(window, kernel[row_tap, col_tap], preferred_element_type=jnp.floa...  12.5 us
    dot_general x27, matrix products, conv_same(): jnp.dot(window, kernel[row_tap, col_tap], preferred_element_type=jnp.floa...  10.1 us
  transfers between devices with their start and end apart: 17, of which 4 were waited for; matrix products, arithmetic and copies ran while one was open for 7% of the time, Pallas kernels for 0%

commit v1 on v0

--- a/solution.py
+++ b/solution.py
@@ -5,6 +5,11 @@
 from jax.sharding import PartitionSpec as P
 
 MARGIN = 8
+
+
+def one_after_other(value, one, other):
+    inner = lax.psum(value, one)
+    return lax.psum(inner, other)
 
 
 def passed_along(block, axis, distance):
@@ -168,9 +173,10 @@
         empty, d_patch.astype(jnp.float32), (start_r, start_c, zero)
     )
     field_grad = return_margins(d_canvas, tile_h, tile_w, edge)
-    g_first, g_down, g_up = lax.psum(
+    g_first, g_down, g_up = one_after_other(
         (d_first.astype(jnp.float32), d_down.astype(jnp.float32), d_up.astype(jnp.float32)),
-        ("col", "row"),
+        "row",
+        "col",
     )
     scale = 1.0 / math.sqrt(tile_h * rows_n * tile_w * cols_n)
     return (blended, field_grad, g_first * scale, g_down * scale, g_up * scale)

time: 502 us -> 936 us (1.86)
  the two profiles are of different devices: /device:TPU:17 before, /device:TPU:2 now
where the time goes in v1:
time: 936 us; the launch traced here: 934 us
  waiting for transfers between devices  743 us (79%)
  starting transfers between devices  56.9 us (6%)
  local copies, waits for them, and re-layouts  54.4 us (6%)
  matrix products  33.8 us (4%)
  between operations  29.6 us (3%)
  other arithmetic  16.2 us (2%)
    psum x1, waiting for transfers between devices, one_after_other(): return lax.psum(inner, other)  497 us
    psum x1, waiting for transfers between devices, one_after_other(): inner = lax.psum(value, one)  220 us
    unnamed x82, local copies, waits for them, and re-layouts  31.7 us
    ppermute x8, starting transfers between devices, passed_along(): return lax.ppermute(block, axis, route)  26.5 us
    ppermute x4, starting transfers between devices, extended(): before = lax.ppermute(last, axis, up)  22.7 us
    ppermute x8, waiting for transfers between devices, passed_along(): return lax.ppermute(block, axis, route)  19.4 us
  transfers between devices with their start and end apart: 18, of which 7 were waited for; matrix products, arithmetic and copies ran while one was open for 3% of the time, Pallas kernels for 0%

profile of v1, /device:TPU:2, one launch (start us, length us, event | category | flops | bytes accessed | tf_op | source)
XLA Modules:
  0.0 933.9 jit_solution(15904743447958515720)
XLA Ops:
  7.2 10.9 %collective-permute-start = (bf16[16,16,128]{2,1,0:T(8,128)(2,1)}, bf16[16,16,128]{2,1,0:T(8,128)(2,1)S(1)}, u32[]{:S(2)}, u32[]{:S(2)}) collective-permute-start(bf16[16,16,128]{2,1,0:T(8,128)(2,1)} %param.23), channel_id=1, source_target_pairs={{0,1},{1,2},{2,3},{3,4},{4,5},{5,6},{6,7},{8,9},{9,10},{10,11},{11... | collective-permute-start | bytes 196616 | tf_op jit(solution)/shard_map/ppermute | solution.py:28
  18.2 1.9 collective-permute-start.1
  20.1 1.0 constant_dynamic-slice_fusion
  24.1 0.9 fusion.167
  25.0 0.9 fusion.168
  27.2 0.9 fusion.169
  30.0 0.9 fusion.170
  32.1 0.9 fusion.171
  34.9 0.9 fusion.172
  37.1 0.9 fusion.173
  39.8 0.9 fusion.174
  42.0 0.9 fusion.175
  45.5 1.5 collective-permute-start.2
  47.0 1.3 collective-permute-start.3
  48.4 7.7 collective-permute-start.8
  56.1 3.0 collective-permute-start.9
  61.7 6.3 collective-permute-done.9
  68.8 2.6 collective-permute-start.10
  71.4 1.3 collective-permute-start.11
  83.3 2.3 convert_multiply_fusion.2
  102.0 5.6 pad.345
  107.6 8.5 pad.348
  116.1 8.4 pad.346
  124.5 5.6 pad.347
  130.1 5.6 pad.214
  135.7 5.6 pad.215
  142.3 1.8 fusion.52
  147.9 1.2 add_convert_fusion
  149.0 0.9 add_convert_fusion.1
  150.6 0.9 convolution_convert_fusion.6
  152.7 220.4 %all-reduce.49.cloned.1.call-done = (f32[3,3,128,128]{3,2,1,0:T(8,128)}, f32[3,3,128,256]{3,2,1,0:T(8,128)}, f32[2,2,256,128]{3,2,1,0:T(8,128)}) async-done(((f32[3,3,128,128]{3,2,1,0:T(8,128)}, f32[3,3,128,256]{3,2,1,0:T(8,128)}, f32[2,2,256,128]{3,2,1,0:T(8,128)}), (f32[3,3,128,128]{3,2,1,0:T(8,128)}, f32[3,3,128,256]{3,2,1,0:T(8,128)}, f32[2,2,256,128]{3,2,1,0:T(8,128)})) %all-reduce.49.cloned.1.call-update) | async-done | bytes 2293776 | tf_op jit(solution)/shard_map/psum | solution.py:11
  373.4 1.2 pad_add_fusion
  375.2 1.3 dynamic_update_slice.7
  376.7 1.3 dynamic_update_slice.6
  378.1 4.6 collective-permute-start.4
  382.7 6.0 collective-permute-start.5
  388.8 3.7 collective-permute-start.12
  392.5 6.9 collective-permute-start.13
  399.4 1.2 collective-permute-done.5
  400.7 1.3 collective-permute-start.6
  402.0 1.3 collective-permute-start.7
  403.3 8.6 collective-permute-done.12
  411.9 2.1 collective-permute-done.13
  414.1 1.3 collective-permute-start.14
  415.5 1.3 collective-permute-start.15
  417.5 7.5 collective-permute-done.15
  425.7 496.9 %all-reduce.47.cloned.1.call-done = (f32[3,3,128,128]{3,2,1,0:T(8,128)}, f32[3,3,128,256]{3,2,1,0:T(8,128)}, f32[2,2,256,128]{3,2,1,0:T(8,128)}) async-done(((f32[3,3,128,128]{3,2,1,0:T(8,128)}, f32[3,3,128,256]{3,2,1,0:T(8,128)}, f32[2,2,256,128]{3,2,1,0:T(8,128)}), (f32[3,3,128,128]{3,2,1,0:T(8,128)}, f32[3,3,128,256]{3,2,1,0:T(8,128)}, f32[2,2,256,128]{3,2,1,0:T(8,128)})) %all-reduce.47.cloned.1.call-update) | async-done | bytes 2293776 | tf_op jit(solution)/shard_map/psum | solution.py:12
  922.5 2.4 broadcast_multiply_fusion
  (235 shorter events, 43.2 us)
Async XLA Ops:
  7.2 38.3 %copy-start.35 = (bf16[16,16,128]{2,1,0:T(8,128)(2,1)S(1)}, bf16[16,16,128]{2,1,0:T(8,128)(2,1)}, u32[]{:S(2)}) copy-start(bf16[16,16,128]{2,1,0:T(8,128)(2,1)} %param.23) | copy-start | bytes 196612
  7.2 54.5 %copy-start.37 = (s32[32,32]{1,0:T(8,128)S(1)}, s32[32,32]{1,0:T(8,128)}, u32[]{:S(2)}) copy-start(s32[32,32]{1,0:T(8,128)} %param.29) | copy-start | bytes 12292
  7.2 41.1 %copy-start.36 = (bf16[16,16,128]{2,1,0:T(8,128)(2,1)S(1)}, bf16[16,16,128]{2,1,0:T(8,128)(2,1)}, u32[]{:S(2)}) copy-start(bf16[16,16,128]{2,1,0:T(8,128)(2,1)} %param.24) | copy-start | bytes 196612
  7.2 365.9 %all-reduce.49.cloned.1.call-start = ((), (), s32[]{:S(2)}) async-start(), calls=%async_computation.1 | async-start | bytes 4587520 | tf_op jit(solution)/shard_map/psum | solution.py:11
  7.2 38.2 %collective-permute-start = (bf16[16,16,128]{2,1,0:T(8,128)(2,1)}, bf16[16,16,128]{2,1,0:T(8,128)(2,1)S(1)}, u32[]{:S(2)}, u32[]{:S(2)}) collective-permute-start(bf16[16,16,128]{2,1,0:T(8,128)(2,1)} %param.23), channel_id=1, source_target_pairs={{0,1},{1,2},{2,3},{3,4},{4,5},{5,6},{6,7},{8,9},{9,10},{10,11},{11... | collective-permute-start | bytes 196616 | tf_op jit(solution)/shard_map/ppermute | solution.py:28
  18.2 27.3 %collective-permute-start.1 = (bf16[16,16,128]{2,1,0:T(8,128)(2,1)}, bf16[16,16,128]{2,1,0:T(8,128)(2,1)S(1)}, u32[]{:S(2)}, u32[]{:S(2)}) collective-permute-start(bf16[16,16,128]{2,1,0:T(8,128)(2,1)} %param.23), channel_id=1, source_target_pairs={{1,0},{2,1},{3,2},{4,3},{5,4},{6,5},{7,6},{9,8},{10,9},{11,10},{12... | collective-permute-start | bytes 196616 | tf_op jit(solution)/shard_map/ppermute | solution.py:29
  45.5 27.2 %collective-permute-start.2 = (bf16[48,16,128]{2,1,0:T(8,128)(2,1)S(1)}, bf16[48,16,128]{2,1,0:T(8,128)(2,1)S(1)}, u32[]{:S(2)}, u32[]{:S(2)}) collective-permute-start(bf16[48,16,128]{2,1,0:T(8,128)(2,1)S(1)} %constant_dynamic-update-slice_fusion), channel_id=1, source_target_pairs={{0,8},{8,16},{16,24},{24,32},{32,40},{40,48},{48,56},{56,64},{64,7... | collective-permute-start | bytes 589832 | tf_op jit(solution)/shard_map/ppermute | solution.py:28
  47.0 25.7 %collective-permute-start.3 = (bf16[48,16,128]{2,1,0:T(8,128)(2,1)S(1)}, bf16[48,16,128]{2,1,0:T(8,128)(2,1)S(1)}, u32[]{:S(2)}, u32[]{:S(2)}) collective-permute-start(bf16[48,16,128]{2,1,0:T(8,128)(2,1)S(1)} %constant_dynamic-update-slice_fusion), channel_id=1, source_target_pairs={{8,0},{16,8},{24,16},{32,24},{40,32},{48,40},{56,48},{64,56},{72,6... | collective-permute-start | bytes 589832 | tf_op jit(solution)/shard_map/ppermute | solution.py:29
  48.4 13.3 %collective-permute-start.8 = (bf16[16,16,128]{2,1,0:T(8,128)(2,1)S(1)}, bf16[16,16,128]{2,1,0:T(8,128)(2,1)S(1)}, u32[]{:S(2)}, u32[]{:S(2)}) collective-permute-start(bf16[16,16,128]{2,1,0:T(8,128)(2,1)S(1)} %divide_convert_fusion), channel_id=1, source_target_pairs={{0,1},{1,2},{2,3},{3,4},{4,5},{5,6},{6,7},{8,9},{9,10},{10,11},{11... | collective-permute-start | bytes 196616 | tf_op jit(solution)/shard_map/ppermute | solution.py:28
  56.1 12.0 %collective-permute-start.9 = (bf16[16,16,128]{2,1,0:T(8,128)(2,1)S(1)}, bf16[16,16,128]{2,1,0:T(8,128)(2,1)S(1)}, u32[]{:S(2)}, u32[]{:S(2)}) collective-permute-start(bf16[16,16,128]{2,1,0:T(8,128)(2,1)S(1)} %divide_convert_fusion), channel_id=1, source_target_pairs={{1,0},{2,1},{3,2},{4,3},{5,4},{6,5},{7,6},{9,8},{10,9},{11,10},{12... | collective-permute-start | bytes 196616 | tf_op jit(solution)/shard_map/ppermute | solution.py:29
  61.7 11.6 %copy-start.28 = (bf16[16,16,128]{2,1,0:T(8,128)(2,1)}, bf16[16,16,128]{2,1,0:T(8,128)(2,1)S(1)}, u32[]{:S(2)}) copy-start(bf16[16,16,128]{2,1,0:T(8,128)(2,1)S(1)} %collective-permute-done.8) | copy-start | bytes 196612
  68.1 5.3 copy-start.30
  68.8 14.2 %collective-permute-start.10 = (bf16[48,16,128]{2,1,0:T(8,128)(2,1)}, bf16[48,16,128]{2,1,0:T(8,128)(2,1)}, u32[]{:S(2)}, u32[]{:S(2)}) collective-permute-start(bf16[48,16,128]{2,1,0:T(8,128)(2,1)} %pad_maximum_fusion.1), channel_id=1, source_target_pairs={{0,8},{8,16},{16,24},{24,32},{32,40},{40,48},{48,56},{56,64},{64,7... | collective-permute-start | bytes 589832 | tf_op jit(solution)/shard_map/ppermute | solution.py:28
  71.4 11.5 %collective-permute-start.11 = (bf16[48,16,128]{2,1,0:T(8,128)(2,1)}, bf16[48,16,128]{2,1,0:T(8,128)(2,1)}, u32[]{:S(2)}, u32[]{:S(2)}) collective-permute-start(bf16[48,16,128]{2,1,0:T(8,128)(2,1)} %pad_maximum_fusion.1), channel_id=1, source_target_pairs={{8,0},{16,8},{24,16},{32,24},{40,32},{48,40},{56,48},{64,56},{72,6... | collective-permute-start | bytes 589832 | tf_op jit(solution)/shard_map/ppermute | solution.py:29
  73.0 1.0 copy-start.1
  75.9 3.8 copy-start
  76.5 3.7 copy-start.13
  78.4 2.1 copy-start.7
  78.8 1.9 copy-start.9
  79.2 1.7 copy-start.11
  79.6 1.5 copy-start.32
  80.7 1.0 copy-start.5
  90.1 1.7 copy-start.12
  90.1 2.5 copy-start.10
  90.1 2.7 copy-start.8
  91.0 6.0 copy-start.14
  102.0 22.5 %copy-start.34 = (bf16[256,128]{1,0:T(8,128)(2,1)S(1)}, bf16[256,128]{1,0:T(8,128)(2,1)}, u32[]{:S(2)}) copy-start(bf16[256,128]{1,0:T(8,128)(2,1)} %convolution_convert_fusion.19) | copy-start | bytes 196612
  141.2 1.0 copy-start.3
  141.2 1.1 copy-start.4
  146.1 1.7 copy-start.16
  146.1 1.7 copy-start.17
  146.1 1.7 copy-start.18
  146.1 1.7 copy-start.19
  146.1 1.7 copy-start.20
  146.1 1.7 copy-start.21
  146.1 1.7 copy-start.22
  146.1 1.7 copy-start.23
  149.9 772.6 %all-reduce.47.cloned.1.call-start = ((), (), s32[]{:S(2)}) async-start(), calls=%async_computation | async-start | bytes 4587520 | tf_op jit(solution)/shard_map/psum | solution.py:12
  378.1 21.4 %collective-permute-start.4 = (bf16[16,48,128]{2,1,0:T(8,128)(2,1)S(1)}, bf16[16,48,128]{2,1,0:T(8,128)(2,1)S(1)}, u32[]{:S(2)}, u32[]{:S(2)}) collective-permute-start(bf16[16,48,128]{2,1,0:T(8,128)(2,1)S(1)} %get-tuple-element.113), channel_id=1, source_target_pairs={{0,1},{1,2},{2,3},{3,4},{4,5},{5,6},{6,7},{8,9},{9,10},{10,11},{11... | collective-permute-start | bytes 589832 | tf_op jit(solution)/shard_map/ppermute | solution.py:18
  382.7 17.9 %collective-permute-start.5 = (bf16[16,48,128]{2,1,0:T(8,128)(2,1)S(1)}, bf16[16,48,128]{2,1,0:T(8,128)(2,1)S(1)}, u32[]{:S(2)}, u32[]{:S(2)}) collective-permute-start(bf16[16,48,128]{2,1,0:T(8,128)(2,1)S(1)} %get-tuple-element.114), channel_id=1, source_target_pairs={{1,0},{2,1},{3,2},{4,3},{5,4},{6,5},{7,6},{9,8},{10,9},{11,10},{12... | collective-permute-start | bytes 589832 | tf_op jit(solution)/shard_map/ppermute | solution.py:18
  388.8 23.1 %collective-permute-start.12 = (bf16[16,48,128]{2,1,0:T(8,128)(2,1)S(1)}, bf16[16,48,128]{2,1,0:T(8,128)(2,1)S(1)}, u32[]{:S(2)}, u32[]{:S(2)}) collective-permute-start(bf16[16,48,128]{2,1,0:T(8,128)(2,1)S(1)} %get-tuple-element.111), channel_id=1, source_target_pairs={{0,1},{1,2},{2,3},{3,4},{4,5},{5,6},{6,7},{8,9},{9,10},{10,11},{11... | collective-permute-start | bytes 589832 | tf_op jit(solution)/shard_map/ppermute | solution.py:18
  392.5 21.5 %collective-permute-start.13 = (bf16[16,48,128]{2,1,0:T(8,128)(2,1)S(1)}, bf16[16,48,128]{2,1,0:T(8,128)(2,1)S(1)}, u32[]{:S(2)}, u32[]{:S(2)}) collective-permute-start(bf16[16,48,128]{2,1,0:T(8,128)(2,1)S(1)} %get-tuple-element.112), channel_id=1, source_target_pairs={{1,0},{2,1},{3,2},{4,3},{5,4},{6,5},{7,6},{9,8},{10,9},{11,10},{12... | collective-permute-start | bytes 589832 | tf_op jit(solution)/shard_map/ppermute | solution.py:18
  400.7 16.0 %collective-permute-start.6 = (bf16[16,16,128]{2,1,0:T(8,128)(2,1)S(1)}, bf16[16,16,128]{2,1,0:T(8,128)(2,1)S(1)}, u32[]{:S(2)}, u32[]{:S(2)}) collective-permute-start(bf16[16,16,128]{2,1,0:T(8,128)(2,1)S(1)} %get-tuple-element.131), channel_id=1, source_target_pairs={{0,8},{8,16},{16,24},{24,32},{32,40},{40,48},{48,56},{56,64},{64,7... | collective-permute-start | bytes 196616 | tf_op jit(solution)/shard_map/ppermute | solution.py:18
  402.0 14.7 %collective-permute-start.7 = (bf16[16,16,128]{2,1,0:T(8,128)(2,1)S(1)}, bf16[16,16,128]{2,1,0:T(8,128)(2,1)S(1)}, u32[]{:S(2)}, u32[]{:S(2)}) collective-permute-start(bf16[16,16,128]{2,1,0:T(8,128)(2,1)S(1)} %get-tuple-element.132), channel_id=1, source_target_pairs={{8,0},{16,8},{24,16},{32,24},{40,32},{48,40},{56,48},{64,56},{72,6... | collective-permute-start | bytes 196616 | tf_op jit(solution)/shard_map/ppermute | solution.py:18
  414.1 3.4 collective-permute-start.14
  415.5 9.5 %collective-permute-start.15 = (bf16[16,16,128]{2,1,0:T(8,128)(2,1)S(1)}, bf16[16,16,128]{2,1,0:T(8,128)(2,1)S(1)}, u32[]{:S(2)}, u32[]{:S(2)}) collective-permute-start(bf16[16,16,128]{2,1,0:T(8,128)(2,1)S(1)} %get-tuple-element.130), channel_id=1, source_target_pairs={{8,0},{16,8},{24,16},{32,24},{40,32},{48,40},{56,48},{64,56},{72,6... | collective-permute-start | bytes 196616 | tf_op jit(solution)/shard_map/ppermute | solution.py:18
  922.5 2.5 copy-start.6
  925.0 1.3 copy-start.15
  (8 other events, 7.0 us)
Sparse Core Ops, SparseCore 0:
  150.1 222.9 all-reduce.48
  376.2 546.2 all-reduce.46
